TPU v7x, 256 devices: a whole 4x4x8 slice. The times are simulated.
256 devices in a mesh: user: 32 (over z, x), tp: 8 (over y, core).
Axes of the slice: x: 4, y: 4, z: 8, core: 2. Of those that a mesh axis runs over, the one named last changes fastest.
Arguments:
- cand_feats: bfloat16 [32768, 1024], P('user', 'tp'), may hold values from -6 to 6
- w_in: bfloat16 [1024, 2048], P(None, 'tp'), may hold values from -0.1875 to 0.1875
- w_out: bfloat16 [1024, 1024], P('tp'), may hold values from -0.1875 to 0.1875
- kv_cache: bfloat16 [2048, 128, 2048], P('user', None, 'tp'), may hold values from -6 to 6
- event_mask: int32 [2048, 128], P('user'), may hold values from 0 to 1, as said below
- block_counts: int32 [256], P('user'), may hold values from 1 to 8, as said below
- user_blocks: int32 [256, 8], P('user'), may hold values from 0 to 63, as said below
- send_slots: int32 [1024, 2], P('user'), may hold values from 0 to 63, as said below
- cand_user: int32 [32768], P('user'), may hold values from 0 to 7
Outputs:
- scored: bfloat16 [32768, 1024], P('user', 'tp')
Inputs may be any that keep to these rules, and one draw needn't show every extreme that they name: `block_counts`: on every index of the user axis some user has 8 blocks, and on one index every user has. For user u of the index r of the user axis and j < block_counts[r * 8 + u], user_blocks[r * 8 + u, j] = o * 2 + c says that block j of u's history is cached on index o, in its local row send_slots[o * 32 + r, c] of kv_cache and event_mask. These valid entries of one index's users are all different, and on one index they take all 64 values. Entries with j >= block_counts[u] are arbitrary. `send_slots`: the 32 rows of one holder o (rows o * 32 to o * 32 + 31) name each of its local rows 0 to 63 exactly once. `event_mask`: in every block of a user's history the first event is real.
All inputs are finite; a program needn't handle non-finite values.
Results may differ from a plain program's by a relative error of at most 0.013.
Values may be sent and summed in bfloat16 or wider, within the bound.
A program may use at most 128 MiB of HBM per device.

v0:
```python
import jax
import jax.numpy as jnp
from jax import lax
from jax.sharding import PartitionSpec as P

DH = 128
EVENTS = 128
norm_eps = 1e-06


def owner_users(block_count, block_table, slot_count):
    user_count, most_blocks = block_table.shape
    live_mask = jnp.arange(most_blocks, dtype=jnp.int32)[None, :] < block_count[:, None]
    slot_hit = (
        block_table[:, :, None] == jnp.arange(slot_count, dtype=jnp.int32)[None, None, :]
    ) & live_mask[:, :, None]
    user_label = jnp.arange(user_count, dtype=jnp.int32)[:, None, None] + 1
    return jnp.sum(jnp.where(slot_hit, user_label, 0), axis=(0, 1)) - 1


def attend(queries, users, key_pairs, marks, owners):
    row_count, heads_here = (queries.shape[0], queries.shape[1])
    block_rows = min(512, row_count)
    pair_rows = key_pairs.reshape(-1, heads_here, 2, DH)
    key_rows = pair_rows[:, :, 0, :]
    value_rows = pair_rows[:, :, 1, :]
    live_mask = marks.reshape(-1, EVENTS).astype(jnp.float32)
    owner_label = owners.astype(jnp.float32)

    def one_block(packed):
        query_block, user_block = packed
        same_user = (user_block.astype(jnp.float32)[:, None] == owner_label[None, :]).astype(
            jnp.float32
        )
        weights = (same_user[:, :, None] * live_mask[None]).reshape(query_block.shape[0], -1)
        scores = jnp.einsum(
            "rhd,ehd->hre", query_block, key_rows, preferred_element_type=jnp.float32
        ) * DH ** (-0.5)
        attn_weights = (jax.nn.silu(scores) * weights[None]).astype(jnp.bfloat16)
        return jnp.einsum(
            "hre,ehd->rhd", attn_weights, value_rows, preferred_element_type=jnp.float32
        )

    result = lax.map(
        one_block, (queries.reshape(-1, block_rows, heads_here, DH), users.reshape(-1, block_rows))
    )
    return result.reshape(row_count, heads_here, DH)


def per_device(
    cand_feats, w_in, w_out, kv_cache, event_mask, block_counts, user_blocks, send_slots, cand_user
):
    row_count = cand_feats.shape[0]
    heads_here = w_out.shape[0] // DH
    projected = jnp.dot(
        lax.all_gather(cand_feats, "tp", axis=1, tiled=True),
        w_in,
        preferred_element_type=jnp.float32,
    )
    activated = jax.nn.silu(projected).reshape(row_count, heads_here, 2, DH)
    queries = activated[:, :, 0, :].astype(jnp.bfloat16)
    gates = activated[:, :, 1, :].astype(jnp.bfloat16)
    peer_count = lax.axis_size("user")
    capacity = send_slots.shape[1]
    slot_users = owner_users(block_counts, user_blocks, peer_count * capacity)
    picked = send_slots.reshape(-1)
    outgoing = kv_cache[picked].reshape(peer_count, capacity, EVENTS, kv_cache.shape[2])
    out_marks = event_mask[picked].reshape(peer_count, capacity, EVENTS).astype(jnp.bfloat16)
    arrived, arrived_marks = (
        lax.all_to_all(outgoing, "user", split_axis=0, concat_axis=0, tiled=True),
        lax.all_to_all(out_marks, "user", split_axis=0, concat_axis=0, tiled=True),
    )
    attended = attend(queries, cand_user, arrived, arrived_marks, slot_users)
    normed = (
        attended
        * lax.rsqrt(jnp.mean(attended * attended, axis=-1, keepdims=True) + norm_eps)
        * gates.astype(jnp.float32)
    )
    hidden = normed.astype(jnp.bfloat16).reshape(row_count, heads_here * DH)
    head_terms = jnp.dot(hidden, w_out, preferred_element_type=jnp.float32)
    summed = lax.psum_scatter(
        head_terms.astype(jnp.bfloat16), "tp", scatter_dimension=1, tiled=True
    ).astype(jnp.float32)
    return (cand_feats.astype(jnp.float32) + summed).astype(jnp.bfloat16)


def solution(mesh):
    in_specs = (
        P("user", "tp"),
        P(None, "tp"),
        P("tp", None),
        P("user", None, "tp"),
        P("user", None),
        P("user"),
        P("user", None),
        P("user", None),
        P("user"),
    )
    out_specs = P("user", "tp")
    return jax.shard_map(
        per_device, mesh=mesh, in_specs=in_specs, out_specs=out_specs, check_vma=False
    )
```

profile of v0, /device:TPU:2, one launch (start us, length us, event | category | flops | bytes accessed | tf_op | source)
XLA Modules:
  0.0 248.5 jit_solution(2677720347667687180)
XLA Ops:
  6.5 0.8 copy.22
  7.5 1.4 gather_fusion.1
  9.5 11.6 %all-to-all-start.1 = ((bf16[32,2,128]{2,1,0:T(2,128)(2,1)}), bf16[32,2,128]{2,1,0:T(2,128)(2,1)S(1)}, u32[]{:S(2)}, u32[]{:S(2)}) async-start(bf16[32,2,128]{2,1,0:T(2,128)(2,1)} %bitcast.14), calls=%async_computation.1 | async-start | bytes 32768 | tf_op jit(solution)/shard_map/all_to_all | solution.py:71
  21.1 5.0 %gather_fusion = bf16[64,128,256]{2,1,0:T(8,128)(2,1)} fusion(bf16[64,128,256]{2,1,0:T(8,128)(2,1)} %param.14, s32[1024]{0:T(1024)S(1)} %pad_clamp_fusion), kind=kCustom, calls=%fused_computation | custom fusion | bytes 8388864 | tf_op jit(solution)/shard_map/gather | solution.py:67
  26.0 3.5 %all-to-all-done.1 = bf16[32,2,128]{2,1,0:T(2,128)(2,1)S(1)} async-done(((bf16[32,2,128]{2,1,0:T(2,128)(2,1)}), bf16[32,2,128]{2,1,0:T(2,128)(2,1)S(1)}, u32[]{:S(2)}, u32[]{:S(2)}) %all-to-all-start.1) | async-done | bytes 16416 | tf_op jit(solution)/shard_map/all_to_all | solution.py:71
  29.5 6.5 %all-to-all-start = ((bf16[32,2,128,256]{3,2,1,0:T(8,128)(2,1)}), bf16[32,2,128,256]{3,2,1,0:T(8,128)(2,1)}, u32[]{:S(2)}, u32[]{:S(2)}) async-start(bf16[32,2,128,256]{3,2,1,0:T(8,128)(2,1)} %bitcast.92), calls=%async_computation | async-start | bytes 8388608 | tf_op jit(solution)/shard_map/all_to_all | solution.py:70
  37.1 32.6 %all-gather.2.cloned.1.call-done = bf16[1024,1024]{1,0:T(8,128)(2,1)} async-done(((bf16[1024,128]{1,0:T(8,128)(2,1)}), bf16[1024,1024]{1,0:T(8,128)(2,1)}) %all-gather.2.cloned.1.call-update) | async-done | bytes 2097168 | tf_op jit(solution)/shard_map/all_gather | solution.py:56
  69.7 2.5 %multiply_convert_fusion = bf16[1024,256]{0,1:T(8,128)(2,1)S(1)} fusion(bf16[1024,1024]{1,0:T(8,128)(2,1)} %all-gather.2.cloned.1.call-done, bf16[1024,256]{1,0:T(8,128)(2,1)S(1)} %copy-done), kind=kOutput, calls=%fused_computation.20 | convolution fusion | flops 538181632 | bytes 3145728 | tf_op jit(solution)/shard_map/dot_general | solution.py:55
  72.2 0.8 copy-done.2
  73.0 0.8 copy.29
  73.8 55.0 %all-to-all-done = bf16[32,2,128,256]{3,2,1,0:T(8,128)(2,1)} async-done(((bf16[32,2,128,256]{3,2,1,0:T(8,128)(2,1)}), bf16[32,2,128,256]{3,2,1,0:T(8,128)(2,1)}, u32[]{:S(2)}, u32[]{:S(2)}) %all-to-all-start) | async-done | bytes 4194336 | tf_op jit(solution)/shard_map/all_to_all | solution.py:70
  128.9 7.0 %reshape.203 = bf16[8192,1,2,128]{3,2,0,1:T(2,128)(2,1)} reshape(bf16[32,2,128,256]{3,2,1,0:T(8,128)(2,1)} %all-to-all-done) | data formatting | bytes 8388608 | tf_op jit(solution)/shard_map/reshape | solution.py:24
  135.8 8.9 %fusion.29 = (bf16[8192,1,1,128]{3,2,0,1:T(2,128)(2,1)S(1)}, bf16[8192,1,1,128]{3,2,0,1:T(2,128)(2,1)S(1)}) fusion(bf16[8192,1,2,128]{3,2,0,1:T(2,128)(2,1)} %reshape.203), kind=kLoop, calls=%fused_computation.37 | loop fusion | bytes 8388608 | tf_op jit(solution)/shard_map/slice | solution.py:26
  144.7 1.9 copy_bitcast_fusion
  146.6 53.2 %while.10 = (s32[]{:T(128)}, f32[2,512,1,128]{3,1,2,0:T(8,128)S(1)}, bf16[2,512,1,128]{3,1,2,0:T(8,128)(2,1)}, bf16[8192,1,128]{2,0,1:T(8,128)(2,1)}, s32[2,512]...) while((s32[]{:T(128)}, ...), condition=%wide.region_2.3_spmd, body=%wide.region_1.2_spmd.sunk | while | flops 2181104128 | bytes 38444384 | solution.py:44
  146.8 7.0 %mul.127 = f32[512,64,128]{2,1,0:T(8,128)} broadcast(f32[512,64]{1,0:T(8,128)S(1)} %compare_convert_fusion.2), dimensions={0,1} | broadcast | bytes 16908288 | tf_op jit(solution)/shard_map/while/body/eval_jaxpr/mul | solution.py:35
  153.8 19.4 %fusion.40 = f32[2,512,1,128]{3,1,2,0:T(8,128)S(1)} fusion(f32[2,512,1,128]{3,1,2,0:T(8,128)S(1)} %get-tuple-element.151, s32[]{:T(128)} %get-tuple-element.150, bf16[8192,1,128]{2,0,1:T(8,128)(2,1)S(1)} %get-tuple-element.166, f32[64,8,64,128]{3,2,1,0:T(8,128)} %bitcast.91, f32[8192]{0:T(1024)S(1)} %bitcast.101, ...), kind=kOutput, calls=%fused_computation.9.clone.1 | convolution fusion | flops 2181038080 | bytes 21398528 | tf_op jit(solution)/shard_map/while/body/eval_jaxpr/hre,ehd->rhd/dot_general | solution.py:40
  173.4 7.0 %mul.127 = f32[512,64,128]{2,1,0:T(8,128)} broadcast(f32[512,64]{1,0:T(8,128)S(1)} %compare_convert_fusion.2), dimensions={0,1} | broadcast | bytes 16908288 | tf_op jit(solution)/shard_map/while/body/eval_jaxpr/mul | solution.py:35
  180.4 19.4 %fusion.40 = f32[2,512,1,128]{3,1,2,0:T(8,128)S(1)} fusion(f32[2,512,1,128]{3,1,2,0:T(8,128)S(1)} %get-tuple-element.151, s32[]{:T(128)} %get-tuple-element.150, bf16[8192,1,128]{2,0,1:T(8,128)(2,1)S(1)} %get-tuple-element.166, f32[64,8,64,128]{3,2,1,0:T(8,128)} %bitcast.91, f32[8192]{0:T(1024)S(1)} %bitcast.101, ...), kind=kOutput, calls=%fused_computation.9.clone.1 | convolution fusion | flops 2181038080 | bytes 21398528 | tf_op jit(solution)/shard_map/while/body/eval_jaxpr/hre,ehd->rhd/dot_general | solution.py:40
  200.3 1.7 convolution_convert_fusion
  202.0 2.6 %copy.25 = bf16[1024,1024]{0,1:T(8,128)(2,1)} copy(bf16[1024,1024]{1,0:T(8,128)(2,1)S(1)} %convolution_convert_fusion) | data formatting | bytes 4194304
  204.6 35.1 %reduce-scatter.4.cloned.1.call-done = bf16[128,1024]{1,0:T(8,128)(2,1)} async-done(((bf16[1024,1024]{1,0:T(8,128)(2,1)}), bf16[128,1024]{1,0:T(8,128)(2,1)}) %reduce-scatter.4.cloned.1.call-update) | async-done | bytes 262160
  239.8 1.1 copy.26
  240.9 0.8 add_convert_fusion
  (37 shorter events, 2.5 us)
Async XLA Ops:
  6.5 63.1 %copy-start = (bf16[1024,256]{1,0:T(8,128)(2,1)S(1)}, bf16[1024,256]{1,0:T(8,128)(2,1)}, u32[]{:S(2)}) copy-start(bf16[1024,256]{1,0:T(8,128)(2,1)} %param.12) | copy-start | bytes 1572868
  9.5 20.1 %all-to-all-start.1 = ((bf16[32,2,128]{2,1,0:T(2,128)(2,1)}), bf16[32,2,128]{2,1,0:T(2,128)(2,1)S(1)}, u32[]{:S(2)}, u32[]{:S(2)}) async-start(bf16[32,2,128]{2,1,0:T(2,128)(2,1)} %bitcast.14), calls=%async_computation.1 | async-start | bytes 32768 | tf_op jit(solution)/shard_map/all_to_all | solution.py:71
  29.5 7.3 %copy-start.5 = (s32[1024]{0:T(1024)S(1)}, s32[1024]{0:T(1024)}, u32[]{:S(2)}) copy-start(s32[1024]{0:T(1024)} %param.19) | copy-start | bytes 12292
  29.5 7.3 %copy-start.6 = (s32[8]{0:T(128)S(1)}, s32[8]{0:T(128)}, u32[]{:S(2)}) copy-start(s32[8]{0:T(128)} %param.16) | copy-start | bytes 100
  29.5 7.4 %copy-start.4 = (s32[8,8]{1,0:T(8,128)S(1)}, s32[8,8]{1,0:T(8,128)}, u32[]{:S(2)}) copy-start(s32[8,8]{1,0:T(8,128)} %param.17) | copy-start | bytes 772
  29.5 99.3 %all-to-all-start = ((bf16[32,2,128,256]{3,2,1,0:T(8,128)(2,1)}), bf16[32,2,128,256]{3,2,1,0:T(8,128)(2,1)}, u32[]{:S(2)}, u32[]{:S(2)}) async-start(bf16[32,2,128,256]{3,2,1,0:T(8,128)(2,1)} %bitcast.92), calls=%async_computation | async-start | bytes 8388608 | tf_op jit(solution)/shard_map/all_to_all | solution.py:70
  36.0 33.6 %all-gather.2.cloned.1.call-start = ((), (), s32[]{:S(2)}) async-start(), calls=%async_computation.3 | async-start | bytes 2359296 | tf_op jit(solution)/shard_map/all_gather | solution.py:56
  36.8 203.0 %reduce-scatter.4.cloned.1.call-start = ((), (), s32[]{:S(2)}) async-start(), calls=%async_computation.4 | async-start | bytes 2359296
  72.2 0.8 copy-start.2
  146.6 53.7 %copy-start.3 = (bf16[128,1024]{1,0:T(8,128)(2,1)S(1)}, bf16[128,1024]{1,0:T(8,128)(2,1)}, u32[]{:S(2)}) copy-start(bf16[128,1024]{1,0:T(8,128)(2,1)} %param.13) | copy-start | bytes 786436
  202.0 38.9 %copy-start.1 = (bf16[1024,128]{1,0:T(8,128)(2,1)S(1)}, bf16[1024,128]{1,0:T(8,128)(2,1)}, u32[]{:S(2)}) copy-start(bf16[1024,128]{1,0:T(8,128)(2,1)} %param.11) | copy-start | bytes 786436
Sparse Core Ops, SparseCore 0:
  38.7 30.9 all-gather.1
  204.7 34.9 reduce-scatter.3
where the time goes:
time: 249 us
  waiting for transfers between devices  127 us (51%)
  local copies, waits for them, and re-layouts  44.6 us (18%)
  matrix products  43 us (17%)
  starting transfers between devices  18.2 us (7%)
  between operations  13.6 us (5%)
    all_to_all x1, waiting for transfers between devices, per_device(): lax.all_to_all(outgoing, 'user', split_axis=0, concat_axis=0, tiled=True)  55 us
    dot_general x2, matrix products, one_block(): jnp.einsum('hre,ehd->rhd', attn_weights, value_rows, preferred_element_ty...  38.9 us
    unnamed x3, waiting for transfers between devices  35.8 us
    all_gather x1, waiting for transfers between devices, per_device(): lax.all_gather(cand_feats, 'tp', axis=1, tiled=True)  32.6 us
    mul x2, local copies, waits for them, and re-layouts, one_block(): same_user[:, :, None] * live_mask[None]  14 us
    all_to_all x1, starting transfers between devices, per_device(): lax.all_to_all(out_marks, 'user', split_axis=0, concat_axis=0, tiled=True)  11.6 us
    slice x1, local copies, waits for them, and re-layouts, attend(): value_rows = pair_rows[:, :, 1, :]  8.89 us
    unnamed x20, local copies, waits for them, and re-layouts  8.03 us
  transfers between devices with their start and end apart: 4, of which 4 were waited for; matrix products, arithmetic and copies ran while one was open for 3% of the time, Pallas kernels for 0%

commit v1 on v0

--- a/solution.py
+++ b/solution.py
@@ -6,6 +6,19 @@
 DH = 128
 EVENTS = 128
 norm_eps = 1e-06
+
+
+def gather_around(x, axis, dim):
+    ways = lax.axis_size(axis)
+    up = [(d, (d + 1) % ways) for d in range(ways)]
+    down = [(d, (d - 1) % ways) for d in range(ways)]
+    earlier, later = ([x], [x])
+    for _ in range(ways // 2):
+        earlier.append(lax.ppermute(earlier[-1], axis, up))
+    for _ in range((ways - 1) // 2):
+        later.append(lax.ppermute(later[-1], axis, down))
+    line = jnp.concatenate([*earlier[::-1], *later[1:]], axis=dim)
+    return jnp.roll(line, (lax.axis_index(axis) - ways // 2) * x.shape[dim], axis=dim)
 
 
 def owner_users(block_count, block_table, slot_count):
@@ -53,9 +66,7 @@
     row_count = cand_feats.shape[0]
     heads_here = w_out.shape[0] // DH
     projected = jnp.dot(
-        lax.all_gather(cand_feats, "tp", axis=1, tiled=True),
-        w_in,
-        preferred_element_type=jnp.float32,
+        gather_around(cand_feats, "tp", 1), w_in, preferred_element_type=jnp.float32
     )
     activated = jax.nn.silu(projected).reshape(row_count, heads_here, 2, DH)
     queries = activated[:, :, 0, :].astype(jnp.bfloat16)

time: 249 us -> 249 us (level)
  starting transfers between devices: 18.2 us -> 27.5 us
  waiting for transfers between devices: 127 us -> 118 us
    all_gather x1 -> x0, waiting for transfers between devices: 32.6 us -> none  [per_device(): lax.all_gather(cand_feats, 'tp', axis=1, tiled=True)]
    ppermute x0 -> x7, waiting for transfers between devices: none -> 18.4 us  [the longest x4 18.3 us: gather_around(): earlier.append(lax.ppermute(earlier[-1], axis, up))]
    ppermute x0 -> x7, starting transfers between devices: none -> 9.37 us  [the longest x3 9.34 us: gather_around(): later.append(lax.ppermute(later[-1], axis, down))]
    all_to_all x1, waiting for transfers between devices: 55 us -> 60.6 us  [per_device(): lax.all_to_all(outgoing, 'user', split_axis=0, concat_axis=0, tiled=True)]
    unnamed x20 -> x37, local copies, waits for them, and re-layouts: 8.03 us -> 9.37 us
    unnamed x3 -> x2, waiting for transfers between devices: 35.8 us -> 35.2 us
  transfers between devices with their start and end apart: 4 -> 10, of which waited for: 4 -> 7; matrix products, arithmetic and copies ran while one was open for 3% -> 3% of each run, Pallas kernels for 0% -> 0%
where the time goes in v1:
time: 249 us; the launch traced here: 248 us
  waiting for transfers between devices  118 us (47%)
  local copies, waits for them, and re-layouts  45.9 us (18%)
  matrix products  41.5 us (17%)
  starting transfers between devices  27.5 us (11%)
  between operations  13.8 us (6%)
    all_to_all x1, waiting for transfers between devices, per_device(): lax.all_to_all(outgoing, 'user', split_axis=0, concat_axis=0, tiled=True)  60.6 us
    dot_general x2, matrix products, one_block(): jnp.einsum('hre,ehd->rhd', attn_weights, value_rows, preferred_element_ty...  38.8 us
    unnamed x2, waiting for transfers between devices  35.2 us
    ppermute x4, waiting for transfers between devices, gather_around(): earlier.append(lax.ppermute(earlier[-1], axis, up))  18.3 us
    mul x2, local copies, waits for them, and re-layouts, one_block(): same_user[:, :, None] * live_mask[None]  14.1 us
    all_to_all x1, starting transfers between devices, per_device(): lax.all_to_all(out_marks, 'user', split_axis=0, concat_axis=0, tiled=True)  11.6 us
    unnamed x37, local copies, waits for them, and re-layouts  9.37 us
    ppermute x3, starting transfers between devices, gather_around(): later.append(lax.ppermute(later[-1], axis, down))  9.34 us
  transfers between devices with their start and end apart: 10, of which 7 were waited for; matrix products, arithmetic and copies ran while one was open for 3% of the time, Pallas kernels for 0%

profile of v1, /device:TPU:2, one launch (start us, length us, event | category | flops | bytes accessed | tf_op | source)
XLA Modules:
  0.0 248.5 jit_solution(8455276338567292851)
XLA Ops:
  7.5 1.4 gather_fusion.1
  9.5 11.6 %all-to-all-start.1 = ((bf16[32,2,128]{2,1,0:T(2,128)(2,1)}), bf16[32,2,128]{2,1,0:T(2,128)(2,1)S(1)}, u32[]{:S(2)}, u32[]{:S(2)}) async-start(bf16[32,2,128]{2,1,0:T(2,128)(2,1)} %bitcast.14), calls=%async_computation.1 | async-start | bytes 32768 | tf_op jit(solution)/shard_map/all_to_all | solution.py:82
  21.1 5.0 %gather_fusion = bf16[64,128,256]{2,1,0:T(8,128)(2,1)} fusion(bf16[64,128,256]{2,1,0:T(8,128)(2,1)} %param.14, s32[1024]{0:T(1024)S(1)} %pad_clamp_fusion), kind=kCustom, calls=%fused_computation | custom fusion | bytes 8388864 | tf_op jit(solution)/shard_map/gather | solution.py:78
  26.1 3.5 %all-to-all-done.1 = bf16[32,2,128]{2,1,0:T(2,128)(2,1)S(1)} async-done(((bf16[32,2,128]{2,1,0:T(2,128)(2,1)}), bf16[32,2,128]{2,1,0:T(2,128)(2,1)S(1)}, u32[]{:S(2)}, u32[]{:S(2)}) %all-to-all-start.1) | async-done | bytes 16416 | tf_op jit(solution)/shard_map/all_to_all | solution.py:82
  29.5 6.5 %all-to-all-start = ((bf16[32,2,128,256]{3,2,1,0:T(8,128)(2,1)}), bf16[32,2,128,256]{3,2,1,0:T(8,128)(2,1)}, u32[]{:S(2)}, u32[]{:S(2)}) async-start(bf16[32,2,128,256]{3,2,1,0:T(8,128)(2,1)} %bitcast.91), calls=%async_computation | async-start | bytes 8388608 | tf_op jit(solution)/shard_map/all_to_all | solution.py:81
  36.2 7.0 %collective-permute-done = bf16[1024,128]{1,0:T(8,128)(2,1)S(1)} collective-permute-done((bf16[1024,128]{1,0:T(8,128)(2,1)S(1)}, bf16[1024,128]{1,0:T(8,128)(2,1)S(1)}, u32[]{:S(2)}, u32[]{:S(2)}) %collective-permute-start) | collective-permute-done | bytes 262176 | tf_op jit(solution)/shard_map/ppermute | solution.py:17
  43.2 3.0 %collective-permute-start.4 = (bf16[1024,128]{1,0:T(8,128)(2,1)S(1)}, bf16[1024,128]{1,0:T(8,128)(2,1)S(1)}, u32[]{:S(2)}, u32[]{:S(2)}) collective-permute-start(bf16[1024,128]{1,0:T(8,128)(2,1)S(1)} %copy-done.1), channel_id=1, source_target_pairs={{0,7},{1,0},{2,1},{3,2},{4,3},{5,4},{6,5},{7,6},{8,15},{9,8},{10,9... | collective-permute-start | bytes 786440 | tf_op jit(solution)/shard_map/ppermute | solution.py:19
  46.1 4.1 %collective-permute-done.1 = bf16[1024,128]{1,0:T(8,128)(2,1)S(1)} collective-permute-done((bf16[1024,128]{1,0:T(8,128)(2,1)S(1)}, bf16[1024,128]{1,0:T(8,128)(2,1)S(1)}, u32[]{:S(2)}, u32[]{:S(2)}) %collective-permute-start.1) | collective-permute-done | bytes 262176 | tf_op jit(solution)/shard_map/ppermute | solution.py:17
  50.2 3.3 %collective-permute-start.5 = (bf16[1024,128]{1,0:T(8,128)(2,1)S(1)}, bf16[1024,128]{1,0:T(8,128)(2,1)S(1)}, u32[]{:S(2)}, u32[]{:S(2)}) collective-permute-start(bf16[1024,128]{1,0:T(8,128)(2,1)S(1)} %collective-permute-done.4), channel_id=1, source_target_pairs={{0,7},{1,0},{2,1},{3,2},{4,3},{5,4},{6,5},{7,6},{8,15},{9,8},{10,9... | collective-permute-start | bytes 786440 | tf_op jit(solution)/shard_map/ppermute | solution.py:19
  53.5 3.7 %collective-permute-done.2 = bf16[1024,128]{1,0:T(8,128)(2,1)S(1)} collective-permute-done((bf16[1024,128]{1,0:T(8,128)(2,1)S(1)}, bf16[1024,128]{1,0:T(8,128)(2,1)S(1)}, u32[]{:S(2)}, u32[]{:S(2)}) %collective-permute-start.2) | collective-permute-done | bytes 262176 | tf_op jit(solution)/shard_map/ppermute | solution.py:17
  57.4 3.1 %collective-permute-start.6 = (bf16[1024,128]{1,0:T(8,128)(2,1)S(1)}, bf16[1024,128]{1,0:T(8,128)(2,1)S(1)}, u32[]{:S(2)}, u32[]{:S(2)}) collective-permute-start(bf16[1024,128]{1,0:T(8,128)(2,1)S(1)} %collective-permute-done.5), channel_id=1, source_target_pairs={{0,7},{1,0},{2,1},{3,2},{4,3},{5,4},{6,5},{7,6},{8,15},{9,8},{10,9... | collective-permute-start | bytes 786440 | tf_op jit(solution)/shard_map/ppermute | solution.py:19
  60.5 3.7 %collective-permute-done.3 = bf16[1024,128]{1,0:T(8,128)(2,1)S(1)} collective-permute-done((bf16[1024,128]{1,0:T(8,128)(2,1)S(1)}, bf16[1024,128]{1,0:T(8,128)(2,1)S(1)}, u32[]{:S(2)}, u32[]{:S(2)}) %collective-permute-start.3) | collective-permute-done | bytes 262176 | tf_op jit(solution)/shard_map/ppermute | solution.py:17
  68.3 60.6 %all-to-all-done = bf16[32,2,128,256]{3,2,1,0:T(8,128)(2,1)} async-done(((bf16[32,2,128,256]{3,2,1,0:T(8,128)(2,1)}), bf16[32,2,128,256]{3,2,1,0:T(8,128)(2,1)}, u32[]{:S(2)}, u32[]{:S(2)}) %all-to-all-start) | async-done | bytes 4194336 | tf_op jit(solution)/shard_map/all_to_all | solution.py:81
  128.9 7.0 %reshape.203 = bf16[8192,1,2,128]{3,2,0,1:T(2,128)(2,1)} reshape(bf16[32,2,128,256]{3,2,1,0:T(8,128)(2,1)} %all-to-all-done) | data formatting | bytes 8388608 | tf_op jit(solution)/shard_map/reshape | solution.py:37
  135.9 8.8 %fusion.34 = (bf16[8192,1,1,128]{3,2,0,1:T(2,128)(2,1)S(1)}, bf16[8192,1,1,128]{3,2,0,1:T(2,128)(2,1)S(1)}) fusion(bf16[8192,1,2,128]{3,2,0,1:T(2,128)(2,1)} %reshape.203), kind=kLoop, calls=%fused_computation.56 | loop fusion | bytes 8388608 | tf_op jit(solution)/shard_map/slice | solution.py:39
  144.6 1.9 copy_bitcast_fusion
  146.5 53.2 %while.10 = (s32[]{:T(128)}, f32[2,512,1,128]{3,1,2,0:T(8,128)S(1)}, bf16[2,512,1,128]{3,1,2,0:T(8,128)(2,1)S(1)}, bf16[8192,1,128]{2,0,1:T(8,128)(2,1)}, s32[2,...) while((s32[]{:T(128)}, ...), condition=%wide.region_2.3_spmd, body=%wide.region_1.2_spmd.sunk | while | flops 2181104128 | bytes 38444384 | solution.py:57
  146.7 7.0 %mul.131 = f32[512,64,128]{2,1,0:T(8,128)} broadcast(f32[512,64]{1,0:T(8,128)S(1)} %compare_convert_fusion.2), dimensions={0,1} | broadcast | bytes 16908288 | tf_op jit(solution)/shard_map/while/body/eval_jaxpr/mul | solution.py:48
  153.7 19.4 %fusion.44 = f32[2,512,1,128]{3,1,2,0:T(8,128)S(1)} fusion(f32[2,512,1,128]{3,1,2,0:T(8,128)S(1)} %get-tuple-element.151, s32[]{:T(128)} %get-tuple-element.150, bf16[8192,1,128]{2,0,1:T(8,128)(2,1)S(1)} %get-tuple-element.166, f32[64,8,64,128]{3,2,1,0:T(8,128)} %bitcast.90, f32[8192]{0:T(1024)S(1)} %bitcast.100, ...), kind=kOutput, calls=%fused_computation.9.clone.1 | convolution fusion | flops 2181038080 | bytes 21398528 | tf_op jit(solution)/shard_map/while/body/eval_jaxpr/hre,ehd->rhd/dot_general | solution.py:53
  173.2 7.0 %mul.131 = f32[512,64,128]{2,1,0:T(8,128)} broadcast(f32[512,64]{1,0:T(8,128)S(1)} %compare_convert_fusion.2), dimensions={0,1} | broadcast | bytes 16908288 | tf_op jit(solution)/shard_map/while/body/eval_jaxpr/mul | solution.py:48
  180.3 19.4 %fusion.44 = f32[2,512,1,128]{3,1,2,0:T(8,128)S(1)} fusion(f32[2,512,1,128]{3,1,2,0:T(8,128)S(1)} %get-tuple-element.151, s32[]{:T(128)} %get-tuple-element.150, bf16[8192,1,128]{2,0,1:T(8,128)(2,1)S(1)} %get-tuple-element.166, f32[64,8,64,128]{3,2,1,0:T(8,128)} %bitcast.90, f32[8192]{0:T(1024)S(1)} %bitcast.100, ...), kind=kOutput, calls=%fused_computation.9.clone.1 | convolution fusion | flops 2181038080 | bytes 21398528 | tf_op jit(solution)/shard_map/while/body/eval_jaxpr/hre,ehd->rhd/dot_general | solution.py:53
  200.1 1.8 convolution_convert_fusion
  201.9 2.6 %copy.25 = bf16[1024,1024]{0,1:T(8,128)(2,1)} copy(bf16[1024,1024]{1,0:T(8,128)(2,1)S(1)} %convolution_convert_fusion) | data formatting | bytes 4194304
  204.6 35.1 %reduce-scatter.4.cloned.1.call-done = bf16[128,1024]{1,0:T(8,128)(2,1)} async-done(((bf16[1024,1024]{1,0:T(8,128)(2,1)}), bf16[128,1024]{1,0:T(8,128)(2,1)}) %reduce-scatter.4.cloned.1.call-update) | async-done | bytes 262160
  (66 shorter events, 8.4 us)
Async XLA Ops:
  6.5 59.1 %copy-start = (bf16[1024,256]{1,0:T(8,128)(2,1)S(1)}, bf16[1024,256]{1,0:T(8,128)(2,1)}, u32[]{:S(2)}) copy-start(bf16[1024,256]{1,0:T(8,128)(2,1)} %param.12) | copy-start | bytes 1572868
  9.5 20.1 %all-to-all-start.1 = ((bf16[32,2,128]{2,1,0:T(2,128)(2,1)}), bf16[32,2,128]{2,1,0:T(2,128)(2,1)S(1)}, u32[]{:S(2)}, u32[]{:S(2)}) async-start(bf16[32,2,128]{2,1,0:T(2,128)(2,1)} %bitcast.14), calls=%async_computation.1 | async-start | bytes 32768 | tf_op jit(solution)/shard_map/all_to_all | solution.py:82
  29.5 6.6 %copy-start.1 = (bf16[1024,128]{1,0:T(8,128)(2,1)S(1)}, bf16[1024,128]{1,0:T(8,128)(2,1)}, u32[]{:S(2)}) copy-start(bf16[1024,128]{1,0:T(8,128)(2,1)} %param.11) | copy-start | bytes 786436
  29.5 20.6 %copy-start.7 = (s32[8]{0:T(128)S(1)}, s32[8]{0:T(128)}, u32[]{:S(2)}) copy-start(s32[8]{0:T(128)} %param.16) | copy-start | bytes 100
  29.5 27.6 %copy-start.5 = (s32[8,8]{1,0:T(8,128)S(1)}, s32[8,8]{1,0:T(8,128)}, u32[]{:S(2)}) copy-start(s32[8,8]{1,0:T(8,128)} %param.17) | copy-start | bytes 772
  29.5 27.8 %copy-start.6 = (s32[1024]{0:T(1024)S(1)}, s32[1024]{0:T(1024)}, u32[]{:S(2)}) copy-start(s32[1024]{0:T(1024)} %param.19) | copy-start | bytes 12292
  29.5 99.3 %all-to-all-start = ((bf16[32,2,128,256]{3,2,1,0:T(8,128)(2,1)}), bf16[32,2,128,256]{3,2,1,0:T(8,128)(2,1)}, u32[]{:S(2)}, u32[]{:S(2)}) async-start(bf16[32,2,128,256]{3,2,1,0:T(8,128)(2,1)} %bitcast.91), calls=%async_computation | async-start | bytes 8388608 | tf_op jit(solution)/shard_map/all_to_all | solution.py:81
  36.1 203.6 %reduce-scatter.4.cloned.1.call-start = ((), (), s32[]{:S(2)}) async-start(), calls=%async_computation.3 | async-start | bytes 2359296
  36.1 7.0 %collective-permute-start = (bf16[1024,128]{1,0:T(8,128)(2,1)S(1)}, bf16[1024,128]{1,0:T(8,128)(2,1)S(1)}, u32[]{:S(2)}, u32[]{:S(2)}) collective-permute-start(bf16[1024,128]{1,0:T(8,128)(2,1)S(1)} %copy-done.1), channel_id=1, source_target_pairs={{0,1},{1,2},{2,3},{3,4},{4,5},{5,6},{6,7},{7,0},{8,9},{9,10},{10,1... | collective-permute-start | bytes 786440 | tf_op jit(solution)/shard_map/ppermute | solution.py:17
  43.2 7.0 %collective-permute-start.1 = (bf16[1024,128]{1,0:T(8,128)(2,1)S(1)}, bf16[1024,128]{1,0:T(8,128)(2,1)S(1)}, u32[]{:S(2)}, u32[]{:S(2)}) collective-permute-start(bf16[1024,128]{1,0:T(8,128)(2,1)S(1)} %collective-permute-done), channel_id=1, source_target_pairs={{0,1},{1,2},{2,3},{3,4},{4,5},{5,6},{6,7},{7,0},{8,9},{9,10},{10,1... | collective-permute-start | bytes 786440 | tf_op jit(solution)/shard_map/ppermute | solution.py:17
  43.2 7.1 %collective-permute-start.4 = (bf16[1024,128]{1,0:T(8,128)(2,1)S(1)}, bf16[1024,128]{1,0:T(8,128)(2,1)S(1)}, u32[]{:S(2)}, u32[]{:S(2)}) collective-permute-start(bf16[1024,128]{1,0:T(8,128)(2,1)S(1)} %copy-done.1), channel_id=1, source_target_pairs={{0,7},{1,0},{2,1},{3,2},{4,3},{5,4},{6,5},{7,6},{8,15},{9,8},{10,9... | collective-permute-start | bytes 786440 | tf_op jit(solution)/shard_map/ppermute | solution.py:19
  50.2 7.0 %collective-permute-start.2 = (bf16[1024,128]{1,0:T(8,128)(2,1)S(1)}, bf16[1024,128]{1,0:T(8,128)(2,1)S(1)}, u32[]{:S(2)}, u32[]{:S(2)}) collective-permute-start(bf16[1024,128]{1,0:T(8,128)(2,1)S(1)} %collective-permute-done.1), channel_id=1, source_target_pairs={{0,1},{1,2},{2,3},{3,4},{4,5},{5,6},{6,7},{7,0},{8,9},{9,10},{10,1... | collective-permute-start | bytes 786440 | tf_op jit(solution)/shard_map/ppermute | solution.py:17
  50.2 7.2 %collective-permute-start.5 = (bf16[1024,128]{1,0:T(8,128)(2,1)S(1)}, bf16[1024,128]{1,0:T(8,128)(2,1)S(1)}, u32[]{:S(2)}, u32[]{:S(2)}) collective-permute-start(bf16[1024,128]{1,0:T(8,128)(2,1)S(1)} %collective-permute-done.4), channel_id=1, source_target_pairs={{0,7},{1,0},{2,1},{3,2},{4,3},{5,4},{6,5},{7,6},{8,15},{9,8},{10,9... | collective-permute-start | bytes 786440 | tf_op jit(solution)/shard_map/ppermute | solution.py:19
  57.2 7.0 %collective-permute-start.3 = (bf16[1024,128]{1,0:T(8,128)(2,1)S(1)}, bf16[1024,128]{1,0:T(8,128)(2,1)S(1)}, u32[]{:S(2)}, u32[]{:S(2)}) collective-permute-start(bf16[1024,128]{1,0:T(8,128)(2,1)S(1)} %collective-permute-done.2), channel_id=1, source_target_pairs={{0,1},{1,2},{2,3},{3,4},{4,5},{5,6},{6,7},{7,0},{8,9},{9,10},{10,1... | collective-permute-start | bytes 786440 | tf_op jit(solution)/shard_map/ppermute | solution.py:17
  57.4 7.4 %collective-permute-start.6 = (bf16[1024,128]{1,0:T(8,128)(2,1)S(1)}, bf16[1024,128]{1,0:T(8,128)(2,1)S(1)}, u32[]{:S(2)}, u32[]{:S(2)}) collective-permute-start(bf16[1024,128]{1,0:T(8,128)(2,1)S(1)} %collective-permute-done.5), channel_id=1, source_target_pairs={{0,7},{1,0},{2,1},{3,2},{4,3},{5,4},{6,5},{7,6},{8,15},{9,8},{10,9... | collective-permute-start | bytes 786440 | tf_op jit(solution)/shard_map/ppermute | solution.py:19
  66.6 0.8 copy-start.3
  144.6 1.9 copy-start.4
  201.9 38.9 %copy-start.2 = (bf16[1024,128]{1,0:T(8,128)(2,1)S(1)}, bf16[1024,128]{1,0:T(8,128)(2,1)}, u32[]{:S(2)}) copy-start(bf16[1024,128]{1,0:T(8,128)(2,1)} %param.11) | copy-start | bytes 786436
Sparse Core Ops, SparseCore 0:
  204.7 34.9 reduce-scatter.3
